TPU v7x, 32 devices: a whole 2x2x4 slice. The times are simulated.
32 devices in a mesh: gx: 8 (over z, y), gy: 4 (over x, core).
Axes of the slice: x: 2, y: 2, z: 4, core: 2. Of those that a mesh axis runs over, the one named last changes fastest.
Arguments:
- fields: float32 [5, 4, 256, 512], P(None, None, 'gx', 'gy'), may hold values from -6 to 6
- viscosity: float32 [4, 256, 512], P(None, 'gx', 'gy'), may hold values from 0.03 to 0.3
- precursor: float32 [5, 4, 512], P(None, None, 'gy'), may hold values from -6 to 6
- tile_index: int32 [512], P('gy'), may hold values from 0 to 511, as said below
- fine_fields: float32 [512, 5, 4, 4, 256], P(('gx', 'gy')), may hold values from -6 to 6
- fine_viscosity: float32 [512, 4, 4, 256], P(('gx', 'gy')), may hold values from 0.03 to 0.3
- partner_gx: int32 [512], P(('gx', 'gy')), may hold values from 0 to 7, as said below
- partner_col: int32 [512], P(('gx', 'gy')), may hold values from 0 to 31
Outputs:
- fields_out: float32 [5, 4, 256, 512], P(None, None, 'gx', 'gy')
- fine_out: float32 [512, 5, 4, 4, 256], P(('gx', 'gy'))
Inputs may be any that keep to these rules, and one draw needn't show every extreme that they name: `tile_index`: inlet cell y takes precursor cell (y + s) mod 512, where s is drawn for each aligned block of 128 cells. `partner_gx`: each device's tiles are glued to outer devices of its own gy row: exactly 2 tiles to each of 8 distinct gx indices; in every gy row one gx index receives 2 tiles from every device of the row.
All inputs are finite; a program needn't handle non-finite values.
Results may differ from a plain program's by a relative error of at most 0.00005.
Values sent between devices are 32-bit elements; how exact they have to be, the bound alone decides.
A program may use at most 64 MiB of HBM per device.

v0:
```python
import functools

import jax
import jax.numpy as jnp
from jax import lax
from jax.experimental import pallas as pl
from jax.experimental.pallas import tpu as pltpu
from jax.sharding import PartitionSpec as P

CAP = 2
LANES = 128

time_step = 0.2
vertical_mix = 0.1
coarse_penalty = 0.5
fine_penalty = 1.0


def lane_take(rows, index):
    return jnp.take_along_axis(rows, index, axis=1, mode="promise_in_bounds")


def kernel(
    ngx, ngy, nfield, levels, columns, tiles, width,
    f_ref, n_ref, p_ref, ti_ref, g_ref, gn_ref, pgx_ref, pcol_ref,
    fo_ref, go_ref,
    tid, col_send, col_recv, ctr, tr_send, tr_recv, an_send, an_recv,
    hx_send, hx_recv, hy_send, hy_recv, pr,
    col_ss, col_rs, tr_ss, tr_rs, an_ss, an_rs, hx_ss, hx_rs, hy_ss, hy_rs, pr_ss, pr_rs,
):
    mx, my = lax.axis_index("gx"), lax.axis_index("gy")
    nz = nfield * levels

    def x_peer(d):
        return (lax.rem(mx + d + ngx, ngx), my)

    def y_peer(d):
        return (mx, lax.rem(my + d + ngy, ngy))

    barrier = pltpu.get_barrier_semaphore()
    for d in range(1, ngx):
        pl.semaphore_signal(barrier, inc=1, device_id=x_peer(d), device_id_type=pl.DeviceIdType.MESH)
    for d in range(1, ngy):
        pl.semaphore_signal(barrier, inc=1, device_id=y_peer(d), device_id_type=pl.DeviceIdType.MESH)

    for d in range(ngx):
        goal = lax.rem(mx + d, ngx)
        first, last = jnp.int32(tiles), jnp.int32(-1)
        for t in range(tiles):
            hit = pgx_ref[t] == goal
            last = jnp.where(hit, t, last)
            u = tiles - 1 - t
            first = jnp.where(pgx_ref[u] == goal, u, first)
        for c, at in enumerate((first, last)):
            inside = jnp.clip(at, 0, tiles - 1)
            tid[d, c] = inside
            value = jnp.where(last < 0, -1, pcol_ref[inside])
            col_send[d, c] = value
            if d == 0:
                col_recv[d, c] = value

    rows = lax.broadcasted_iota(jnp.int32, (columns, LANES), 0)
    lanes = lax.broadcasted_iota(jnp.int32, (columns, LANES), 1)
    lane_z = lax.broadcasted_iota(jnp.int32, (nz, LANES), 1)

    def slab(k):
        return f_ref[k * columns : (k + 1) * columns, :]

    def nslab(z):
        return n_ref[z * columns : (z + 1) * columns, :]

    for side, row in ((0, columns - 1), (1, 0)):
        hx_send[side, 0:nz, :] = f_ref[pl.ds(row, nz, stride=columns), :]
        hx_send[side, nz : nz + levels, :] = n_ref[pl.ds(row, levels, stride=columns), :]
    for side, lane in ((0, LANES - 1), (1, 0)):
        packed = jnp.zeros((columns, LANES), jnp.float32)
        for k in range(nz + levels):
            s = slab(k) if k < nz else nslab(k - nz)
            packed = jnp.where(
                lanes == k, jnp.broadcast_to(s[:, lane : lane + 1], (columns, LANES)), packed
            )
        hy_send[side] = packed
    for f in range(nfield):
        pr[0, f * levels : (f + 1) * levels, :] = p_ref[f]

    pl.semaphore_wait(barrier, ngx + ngy - 2)

    def remote(src, dst, ss, rs, to):
        return pltpu.make_async_remote_copy(
            src_ref=src, dst_ref=dst, send_sem=ss, recv_sem=rs,
            device_id=to, device_id_type=pl.DeviceIdType.MESH,
        )

    col = [remote(col_send.at[d], col_recv.at[d], col_ss.at[d], col_rs.at[d], x_peer(d)) for d in range(1, ngx)]
    for c in col:
        c.start()
    halo = [
        remote(hx_send.at[0], hx_recv.at[0], hx_ss.at[0], hx_rs.at[0], x_peer(1)),
        remote(hx_send.at[1], hx_recv.at[1], hx_ss.at[1], hx_rs.at[1], x_peer(-1)),
        remote(hy_send.at[0], hy_recv.at[0], hy_ss.at[0], hy_rs.at[0], y_peer(1)),
        remote(hy_send.at[1], hy_recv.at[1], hy_ss.at[1], hy_rs.at[1], y_peer(-1)),
    ]
    for c in halo:
        c.start()
    plane = [remote(pr.at[0], pr.at[d], pr_ss.at[d], pr_rs.at[d], y_peer(d)) for d in range(1, ngy)]

    @pl.when(mx == 0)
    def _():
        for c in plane:
            c.start()

    even = (2 * lane_z) % LANES

    def coarsen(t, carry):
        g0 = g_ref[t, pl.ds(0, nz, stride=8), :]
        g1 = g_ref[t, pl.ds(4, nz, stride=8), :]
        r0, r1 = pltpu.roll(g0, 1, 1), pltpu.roll(g1, 1, 1)
        l0 = jnp.where(lane_z == 0, g0, r0)
        l1 = jnp.where(lane_z == 0, r0, r1)
        y0 = 0.5 * g0 + 0.25 * (l0 + pltpu.roll(g0, LANES - 1, 1))
        y1 = 0.5 * g1 + 0.25 * (l1 + pltpu.roll(g1, LANES - 1, 1))
        ctr[t] = jnp.where(lane_z < LANES // 2, lane_take(y0, even), lane_take(y1, even))
        return carry

    lax.fori_loop(0, tiles, coarsen, 0)
    traces = [remote(tr_send.at[d], tr_recv.at[d], tr_ss.at[d], tr_rs.at[d], x_peer(d)) for d in range(1, ngx)]
    for d in range(ngx):
        for c in range(CAP):
            if d == 0:
                tr_recv[0, c] = ctr[tid[0, c]]
            else:
                tr_send[d, c] = ctr[tid[d, c]]
        if d:
            traces[d - 1].start()

    answers = [remote(an_send.at[d], an_recv.at[d], an_ss.at[d], an_rs.at[d], x_peer(-d)) for d in range(1, ngx)]
    for d in range(ngx):
        if d:
            col[d - 1].wait_recv()
        for c in range(CAP):
            at = jnp.maximum(col_recv[d, c], 0)
            for k in range(nz):
                row = f_ref[pl.ds(k * columns + at, 1), :]
                if d:
                    an_send[d, c, k : k + 1, :] = row
                else:
                    an_recv[0, c, k : k + 1, :] = row
        if d:
            answers[d - 1].start()

    row8 = lax.broadcasted_iota(jnp.int32, (8, LANES), 0)
    lane8 = lax.broadcasted_iota(jnp.int32, (8, LANES), 1)
    x_last = (row8 % 4) == 3
    is_glue = (row8 % 4) == 0
    y_last = (lane8 == LANES - 1) & (row8 >= 4)
    lane_last, lane_first = lane8 == LANES - 1, lane8 == 0
    zero = jnp.zeros((8, LANES), jnp.float32)
    own = jnp.where(is_glue, 1.0 - time_step * fine_penalty, 1.0)

    def up_x(q):
        return pltpu.roll(q, 7, 0)

    def down_x(q):
        return pltpu.roll(q, 1, 0)

    def up_y(q):
        r = pltpu.roll(q, LANES - 1, 1)
        return jnp.where(lane_last, pltpu.roll(r, 4, 0), r)

    def down_y(q):
        r = pltpu.roll(q, 1, 1)
        return jnp.where(lane_first, pltpu.roll(r, 4, 0), r)

    def fine(t, carry):
        for z in range(levels):
            n = gn_ref[t, z * 8 : z * 8 + 8, :]
            u = time_step * g_ref[t, z * 8 : z * 8 + 8, :]
            v = time_step * g_ref[t, (levels + z) * 8 : (levels + z) * 8 + 8, :]
            n = (2.0 * time_step) * n
            nx = n + up_x(n)
            ny = n + up_y(n)
            ae, aw = nx - u, down_x(nx) + u
            an, as_ = ny - v, down_y(ny) + v
            for f in range(nfield):
                k = f * levels + z
                q = g_ref[t, k * 8 : k * 8 + 8, :]
                e = jnp.where(x_last, zero, up_x(q) - q)
                w = down_x(e)
                nn = jnp.where(y_last, zero, up_y(q) - q)
                s = down_y(nn)
                out = own * q + ae * e - aw * w + an * nn - as_ * s
                if z < levels - 1:
                    out = out + (time_step * vertical_mix) * (g_ref[t, (k + 1) * 8 : (k + 1) * 8 + 8, :] - q)
                if z > 0:
                    out = out - (time_step * vertical_mix) * (q - g_ref[t, (k - 1) * 8 : (k - 1) * 8 + 8, :])
                go_ref[t, k * 8 : k * 8 + 8, :] = out
        return carry

    lax.fori_loop(0, tiles, fine, 0)

    for c in halo:
        c.wait_recv()

    @pl.when(mx == 0)
    def _():
        for c in plane:
            c.wait_recv()
        index = jnp.broadcast_to(ti_ref[...], (nz, LANES))
        per = LANES // width
        inflow = jnp.zeros((nz, LANES), jnp.float32)
        for b in range(ngy * width // LANES):
            parts = [pr[lax.rem(my - (b * per + i) + ngy, ngy)] for i in range(per)]
            block = parts[0] if per == 1 else jnp.concatenate(parts, axis=1)
            inflow = jnp.where(index // LANES == b, lane_take(block, index % LANES), inflow)
        hx_recv[0, 0:nz, :] = inflow
        hx_recv[0, nz : nz + levels, :] = n_ref[pl.ds(0, levels, stride=columns), :]

    @pl.when(mx == ngx - 1)
    def _():
        hx_recv[1, 0:nz, :] = f_ref[pl.ds(columns - 1, nz, stride=columns), :]
        hx_recv[1, nz : nz + levels, :] = n_ref[pl.ds(columns - 1, levels, stride=columns), :]

    for c in traces:
        c.wait_recv()
    count = jnp.zeros((columns, LANES), jnp.float32)
    for d in range(ngx):
        for c in range(CAP):
            count = count + jnp.where(rows == col_recv[d, c], 1.0, 0.0)
    keep = 1.0 - (time_step * coarse_penalty) * count

    def glue(k, carry):
        total = jnp.zeros((columns, LANES), jnp.float32)
        for d in range(ngx):
            for c in range(CAP):
                row = tr_recv[d, c, pl.ds(k, 1), :]
                total = total + jnp.where(
                    rows == col_recv[d, c], jnp.broadcast_to(row, (columns, LANES)), 0.0
                )
        at = pl.multiple_of(k * columns, columns)
        fo_ref[pl.ds(at, columns), :] = (
            keep * f_ref[pl.ds(at, columns), :] + (time_step * coarse_penalty) * total
        )
        return carry

    lax.fori_loop(0, nz, glue, 0)

    def around(q, k):
        e = jnp.where(rows == columns - 1, hx_recv[1, k : k + 1, :], pltpu.roll(q, columns - 1, 0))
        w = jnp.where(rows == 0, hx_recv[0, k : k + 1, :], pltpu.roll(q, 1, 0))
        n = jnp.where(lanes == LANES - 1, hy_recv[1, :, k : k + 1], pltpu.roll(q, LANES - 1, 1))
        s = jnp.where(lanes == 0, hy_recv[0, :, k : k + 1], pltpu.roll(q, 1, 1))
        return e, w, n, s

    half = 0.5 * time_step
    for z in range(levels):
        n = nslab(z)
        ne, nw, nn, ns = around(n, nz + z)
        u, v = slab(z), slab(levels + z)
        ae, aw = half * (n + ne - u), half * (n + nw + u)
        an, as_ = half * (n + nn - v), half * (n + ns + v)
        for f in range(nfield):
            k = f * levels + z
            q = slab(k)
            e, w, north, south = around(q, k)
            out = ae * (e - q) - aw * (q - w) + an * (north - q) - as_ * (q - south)
            if z < levels - 1:
                out = out + (time_step * vertical_mix) * (slab(k + 1) - q)
            if z > 0:
                out = out - (time_step * vertical_mix) * (q - slab(k - 1))
            at = k * columns
            fo_ref[at : at + columns, :] = fo_ref[at : at + columns, :] + out

    for c in answers:
        c.wait_recv()
    low = lane_z // 2
    low_up = low + lane_z % 2
    high = low + LANES // 2
    high_up = jnp.minimum(low_up + LANES // 2, LANES - 1)

    def settle(t, carry):
        goal = pgx_ref[t]
        d = lax.rem(goal - mx + ngx, ngx)
        c = jnp.where(tid[d, 0] == t, 0, 1)
        a = (0.5 * time_step * fine_penalty) * an_recv[d, c]
        r0 = lane_take(a, low) + lane_take(a, low_up)
        r1 = lane_take(a, high) + lane_take(a, high_up)
        for k in range(nz):
            b0 = jnp.broadcast_to(r0[k : k + 1, :], (8, LANES))
            b1 = jnp.broadcast_to(r1[k : k + 1, :], (8, LANES))
            add = jnp.where(is_glue, jnp.where(row8 < 4, b0, b1), zero)
            go_ref[t, k * 8 : k * 8 + 8, :] = go_ref[t, k * 8 : k * 8 + 8, :] + add
        return carry

    lax.fori_loop(0, tiles, settle, 0)

    for c in col + halo + traces + answers:
        c.wait_send()

    @pl.when(mx == 0)
    def _():
        for c in plane:
            c.wait_send()


def halves_in(a):
    lead = a.shape[:-2]
    a = a.reshape(lead + (a.shape[-2], 2, LANES))
    a = jnp.swapaxes(a, -3, -2)
    return a.reshape(lead + (2 * a.shape[-2], LANES))


def halves_out(a):
    lead = a.shape[:-2]
    a = a.reshape(lead + (2, a.shape[-2] // 2, LANES))
    a = jnp.swapaxes(a, -3, -2)
    return a.reshape(lead + (a.shape[-3], 2 * LANES))


def on_device(
    fields, viscosity, precursor, tile_index, fine_fields, fine_viscosity, partner_gx, partner_col
):
    ngx, ngy = lax.axis_size("gx"), lax.axis_size("gy")
    nfield, levels, columns, span = fields.shape
    nz = nfield * levels
    tiles = fine_fields.shape[0]
    width = precursor.shape[2]
    f32, i32 = jnp.float32, jnp.int32
    g = halves_in(fine_fields).reshape(tiles, nz * 8, LANES)
    gn = halves_in(fine_viscosity).reshape(tiles, levels * 8, LANES)
    vmem = pl.BlockSpec(memory_space=pltpu.VMEM)
    smem = pl.BlockSpec(memory_space=pltpu.SMEM)
    dma = pltpu.SemaphoreType.DMA
    trace = pltpu.VMEM((ngx, CAP, nz, LANES), f32)
    fo, go = pl.pallas_call(
        functools.partial(kernel, ngx, ngy, nfield, levels, columns, tiles, width),
        out_shape=(
            jax.ShapeDtypeStruct((nz * columns, span), f32),
            jax.ShapeDtypeStruct((tiles, nz * 8, LANES), f32),
        ),
        in_specs=[vmem] * 6 + [smem] * 2,
        out_specs=(vmem, vmem),
        scratch_shapes=[
            pltpu.SMEM((ngx, CAP), i32),
            pltpu.SMEM((ngx, LANES), i32),
            pltpu.SMEM((ngx, LANES), i32),
            pltpu.VMEM((tiles, nz, LANES), f32),
            trace, trace, trace, trace,
            pltpu.VMEM((2, nz + levels, LANES), f32),
            pltpu.VMEM((2, nz + levels, LANES), f32),
            pltpu.VMEM((2, columns, LANES), f32),
            pltpu.VMEM((2, columns, LANES), f32),
            pltpu.VMEM((ngy, nz, width), f32),
            dma((ngx,)), dma((ngx,)), dma((ngx,)), dma((ngx,)), dma((ngx,)), dma((ngx,)),
            dma((2,)), dma((2,)), dma((2,)), dma((2,)), dma((ngy,)), dma((ngy,)),
        ],
        compiler_params=pltpu.CompilerParams(
            collective_id=0, has_side_effects=True, vmem_limit_bytes=40 * 2**20
        ),
    )(
        fields.reshape(nz * columns, span),
        viscosity.reshape(levels * columns, span),
        precursor,
        tile_index.reshape(1, -1),
        g, gn, partner_gx, partner_col,
    )
    fine_out = halves_out(go.reshape(tiles, nfield, levels, 8, LANES))
    return fo.reshape(fields.shape), fine_out


def solution(mesh):
    return jax.shard_map(
        on_device,
        mesh=mesh,
        in_specs=(
            P(None, None, "gx", "gy"),
            P(None, "gx", "gy"),
            P(None, None, "gy"),
            P("gy"),
            P(("gx", "gy"), None, None, None, None),
            P(("gx", "gy"), None, None, None),
            P(("gx", "gy")),
            P(("gx", "gy")),
        ),
        out_specs=(P(None, None, "gx", "gy"), P(("gx", "gy"), None, None, None, None)),
        check_vma=False,
    )
```

profile of v0, /device:TPU:0, one launch (start us, length us, event | category | flops | bytes accessed | tf_op | source)
XLA Modules:
  0.0 29.2 jit_solution(1723100890200777411)
XLA Ops:
  0.6 0.0 copy-start
  0.6 1.3 %copy-done = f32[16,5,4,4,256]{4,3,2,1,0:T(4,128)S(1)} copy-done((f32[16,5,4,4,256]{4,3,2,1,0:T(4,128)S(1)}, f32[16,5,4,4,256]{4,3,2,1,0:T(4,128)}, u32[]{:S(2)}) %copy-start) | copy-done | bytes 1310744
  1.9 0.0 copy-start.1
  2.0 1.0 %copy-done.1 = f32[5,4,32,128]{3,2,1,0:T(8,128)S(1)} copy-done((f32[5,4,32,128]{3,2,1,0:T(8,128)S(1)}, f32[5,4,32,128]{3,2,1,0:T(8,128)}, u32[]{:S(2)}) %copy-start.1) | copy-done | bytes 327704
  2.9 0.0 copy-start.2
  2.9 0.9 %copy-done.2 = f32[16,4,4,256]{3,2,1,0:T(4,128)S(1)} copy-done((f32[16,4,4,256]{3,2,1,0:T(4,128)S(1)}, f32[16,4,4,256]{3,2,1,0:T(4,128)}, u32[]{:S(2)}) %copy-start.2) | copy-done | bytes 262168
  3.9 0.0 copy-start.3
  3.9 0.8 %copy-done.3 = f32[4,32,128]{2,1,0:T(8,128)S(1)} copy-done((f32[4,32,128]{2,1,0:T(8,128)S(1)}, f32[4,32,128]{2,1,0:T(8,128)}, u32[]{:S(2)}) %copy-start.3) | copy-done | bytes 65560
  4.7 0.0 copy-start.4
  4.7 0.7 %copy-done.4 = f32[5,4,128]{2,1,0:T(4,128)S(1)} copy-done((f32[5,4,128]{2,1,0:T(4,128)S(1)}, f32[5,4,128]{2,1,0:T(4,128)}, u32[]{:S(2)}) %copy-start.4) | copy-done | bytes 10264
  5.4 0.0 copy-start.5
  5.4 0.7 %copy-done.5 = s32[128]{0:T(128)S(1)} copy-done((s32[128]{0:T(128)S(1)}, s32[128]{0:T(128)}, u32[]{:S(2)}) %copy-start.5) | copy-done | bytes 536
  6.1 0.0 copy-start.6
  6.1 0.7 %copy-done.6 = s32[16]{0:T(128)S(1)} copy-done((s32[16]{0:T(128)S(1)}, s32[16]{0:T(128)}, u32[]{:S(2)}) %copy-start.6) | copy-done | bytes 88
  6.7 0.0 copy-start.7
  6.7 0.7 %copy-done.7 = s32[16]{0:T(128)S(1)} copy-done((s32[16]{0:T(128)S(1)}, s32[16]{0:T(128)}, u32[]{:S(2)}) %copy-start.7) | copy-done | bytes 88
  7.4 20.1 %shard_map.95 = (f32[640,128]{1,0:T(8,128)S(1)}, f32[16,160,128]{2,1,0:T(8,128)S(1)}) custom-call(f32[640,128]{1,0:T(8,128)S(1)} %bitcast.21, f32[128,128]{1,0:T(8,128)S(1)} %bitcast.24, f32[5,4,128]{2,1,0:T(4,128)S(1)} %copy-done.4, s32[1,128]{1,0:T(1,128)S(1)} %bitcast.25, f32[16,160,128]{2,1,0:T(8,128)S(1)} %bitcast.19, f32[16,32,128]{2,1,0:T(8,128)S(1)} %bitcast.23, ...), custom_call_target="tpu_custom_call" | custom-call | tf_op jit(solution)/shard_map/pallas_call | solution.py:334
  27.5 0.7 %copy.15 = f32[5,4,32,128]{3,2,1,0:T(8,128)} copy(f32[5,4,32,128]{3,2,1,0:T(8,128)S(1)} %bitcast.22) | data formatting | bytes 655360
  28.2 1.1 %copy.16 = f32[16,5,4,4,256]{4,3,2,1,0:T(4,128)} copy(f32[16,5,4,4,256]{4,3,2,1,0:T(4,128)S(1)} %bitcast.20) | data formatting | bytes 2621440
Async XLA Ops:
  0.6 1.3 %copy-start = (f32[16,5,4,4,256]{4,3,2,1,0:T(4,128)S(1)}, f32[16,5,4,4,256]{4,3,2,1,0:T(4,128)}, u32[]{:S(2)}) copy-start(f32[16,5,4,4,256]{4,3,2,1,0:T(4,128)} %param.12) | copy-start | bytes 3932164
  1.9 1.0 %copy-start.1 = (f32[5,4,32,128]{3,2,1,0:T(8,128)S(1)}, f32[5,4,32,128]{3,2,1,0:T(8,128)}, u32[]{:S(2)}) copy-start(f32[5,4,32,128]{3,2,1,0:T(8,128)} %param.8) | copy-start | bytes 983044
  2.9 0.9 %copy-start.2 = (f32[16,4,4,256]{3,2,1,0:T(4,128)S(1)}, f32[16,4,4,256]{3,2,1,0:T(4,128)}, u32[]{:S(2)}) copy-start(f32[16,4,4,256]{3,2,1,0:T(4,128)} %param.13) | copy-start | bytes 786436
  3.9 0.8 %copy-start.3 = (f32[4,32,128]{2,1,0:T(8,128)S(1)}, f32[4,32,128]{2,1,0:T(8,128)}, u32[]{:S(2)}) copy-start(f32[4,32,128]{2,1,0:T(8,128)} %param.9) | copy-start | bytes 196612
  4.7 0.7 %copy-start.4 = (f32[5,4,128]{2,1,0:T(4,128)S(1)}, f32[5,4,128]{2,1,0:T(4,128)}, u32[]{:S(2)}) copy-start(f32[5,4,128]{2,1,0:T(4,128)} %p_ref.1) | copy-start | bytes 30724
  5.4 0.7 %copy-start.5 = (s32[128]{0:T(128)S(1)}, s32[128]{0:T(128)}, u32[]{:S(2)}) copy-start(s32[128]{0:T(128)} %param.11) | copy-start | bytes 1540
  6.1 0.7 %copy-start.6 = (s32[16]{0:T(128)S(1)}, s32[16]{0:T(128)}, u32[]{:S(2)}) copy-start(s32[16]{0:T(128)} %pgx_ref.1) | copy-start | bytes 196
  6.7 0.7 %copy-start.7 = (s32[16]{0:T(128)S(1)}, s32[16]{0:T(128)}, u32[]{:S(2)}) copy-start(s32[16]{0:T(128)} %pcol_ref.1) | copy-start | bytes 196
where the time goes:
time: 29.6 us; the launch traced here: 29.2 us
  Pallas kernels  20.1 us (68%)
  local copies, waits for them, and re-layouts  8.52 us (29%)
  between operations  0.66 us (2%)
    pallas_call x1, Pallas kernels, on_device(): pl.pallas_call(functools.partial(kernel, ngx, ngy, nfield, levels, column...  20.1 us
    unnamed x18, local copies, waits for them, and re-layouts  8.52 us

commit v1 on v0

--- a/solution.py
+++ b/solution.py
@@ -22,8 +22,9 @@
 
 def kernel(
     ngx, ngy, nfield, levels, columns, tiles, width,
-    f_ref, n_ref, p_ref, ti_ref, g_ref, gn_ref, pgx_ref, pcol_ref,
+    f_hbm, n_hbm, p_hbm, ti_hbm, g_hbm, gn_hbm, pgx_hbm, pcol_hbm,
     fo_ref, go_ref,
+    f_ref, n_ref, p_ref, ti_ref, g_ref, gn_ref, pgx_ref, pcol_ref, in_sems,
     tid, col_send, col_recv, ctr, tr_send, tr_recv, an_send, an_recv,
     hx_send, hx_recv, hy_send, hy_recv, pr,
     col_ss, col_rs, tr_ss, tr_rs, an_ss, an_rs, hx_ss, hx_rs, hy_ss, hy_rs, pr_ss, pr_rs,
@@ -42,6 +43,20 @@
         pl.semaphore_signal(barrier, inc=1, device_id=x_peer(d), device_id_type=pl.DeviceIdType.MESH)
     for d in range(1, ngy):
         pl.semaphore_signal(barrier, inc=1, device_id=y_peer(d), device_id_type=pl.DeviceIdType.MESH)
+
+    pgx_in, pcol_in, f_in, n_in, g_in, gn_in, p_in, ti_in = (
+        pltpu.make_async_copy(src, dst, in_sems.at[i])
+        for i, (src, dst) in enumerate(
+            (
+                (pgx_hbm, pgx_ref), (pcol_hbm, pcol_ref), (f_hbm, f_ref), (n_hbm, n_ref),
+                (g_hbm, g_ref), (gn_hbm, gn_ref), (p_hbm, p_ref), (ti_hbm, ti_ref),
+            )
+        )
+    )
+    for c in (pgx_in, pcol_in, f_in, n_in, g_in, gn_in, p_in, ti_in):
+        c.start()
+    pgx_in.wait()
+    pcol_in.wait()
 
     for d in range(ngx):
         goal = lax.rem(mx + d, ngx)
@@ -59,6 +74,18 @@
             if d == 0:
                 col_recv[d, c] = value
 
+    pl.semaphore_wait(barrier, ngx + ngy - 2)
+
+    def remote(src, dst, ss, rs, to):
+        return pltpu.make_async_remote_copy(
+            src_ref=src, dst_ref=dst, send_sem=ss, recv_sem=rs,
+            device_id=to, device_id_type=pl.DeviceIdType.MESH,
+        )
+
+    col = [remote(col_send.at[d], col_recv.at[d], col_ss.at[d], col_rs.at[d], x_peer(d)) for d in range(1, ngx)]
+    for c in col:
+        c.start()
+
     rows = lax.broadcasted_iota(jnp.int32, (columns, LANES), 0)
     lanes = lax.broadcasted_iota(jnp.int32, (columns, LANES), 1)
     lane_z = lax.broadcasted_iota(jnp.int32, (nz, LANES), 1)
@@ -69,6 +96,8 @@
     def nslab(z):
         return n_ref[z * columns : (z + 1) * columns, :]
 
+    f_in.wait()
+    n_in.wait()
     for side, row in ((0, columns - 1), (1, 0)):
         hx_send[side, 0:nz, :] = f_ref[pl.ds(row, nz, stride=columns), :]
         hx_send[side, nz : nz + levels, :] = n_ref[pl.ds(row, levels, stride=columns), :]
@@ -80,20 +109,9 @@
                 lanes == k, jnp.broadcast_to(s[:, lane : lane + 1], (columns, LANES)), packed
             )
         hy_send[side] = packed
+    p_in.wait()
     for f in range(nfield):
         pr[0, f * levels : (f + 1) * levels, :] = p_ref[f]
-
-    pl.semaphore_wait(barrier, ngx + ngy - 2)
-
-    def remote(src, dst, ss, rs, to):
-        return pltpu.make_async_remote_copy(
-            src_ref=src, dst_ref=dst, send_sem=ss, recv_sem=rs,
-            device_id=to, device_id_type=pl.DeviceIdType.MESH,
-        )
-
-    col = [remote(col_send.at[d], col_recv.at[d], col_ss.at[d], col_rs.at[d], x_peer(d)) for d in range(1, ngx)]
-    for c in col:
-        c.start()
     halo = [
         remote(hx_send.at[0], hx_recv.at[0], hx_ss.at[0], hx_rs.at[0], x_peer(1)),
         remote(hx_send.at[1], hx_recv.at[1], hx_ss.at[1], hx_rs.at[1], x_peer(-1)),
@@ -109,6 +127,7 @@
         for c in plane:
             c.start()
 
+    g_in.wait()
     even = (2 * lane_z) % LANES
 
     def coarsen(t, carry):
@@ -122,7 +141,7 @@
         ctr[t] = jnp.where(lane_z < LANES // 2, lane_take(y0, even), lane_take(y1, even))
         return carry
 
-    lax.fori_loop(0, tiles, coarsen, 0)
+    lax.fori_loop(0, tiles, coarsen, 0, unroll=8)
     traces = [remote(tr_send.at[d], tr_recv.at[d], tr_ss.at[d], tr_rs.at[d], x_peer(d)) for d in range(1, ngx)]
     for d in range(ngx):
         for c in range(CAP):
@@ -155,7 +174,8 @@
     y_last = (lane8 == LANES - 1) & (row8 >= 4)
     lane_last, lane_first = lane8 == LANES - 1, lane8 == 0
     zero = jnp.zeros((8, LANES), jnp.float32)
-    own = jnp.where(is_glue, 1.0 - time_step * fine_penalty, 1.0)
+    mix = time_step * vertical_mix
+    own = [jnp.where(is_glue, 1.0 - time_step * fine_penalty, 1.0) - mix * m for m in range(3)]
 
     def up_x(q):
         return pltpu.roll(q, 7, 0)
@@ -188,16 +208,17 @@
                 w = down_x(e)
                 nn = jnp.where(y_last, zero, up_y(q) - q)
                 s = down_y(nn)
-                out = own * q + ae * e - aw * w + an * nn - as_ * s
-                if z < levels - 1:
-                    out = out + (time_step * vertical_mix) * (g_ref[t, (k + 1) * 8 : (k + 1) * 8 + 8, :] - q)
-                if z > 0:
-                    out = out - (time_step * vertical_mix) * (q - g_ref[t, (k - 1) * 8 : (k - 1) * 8 + 8, :])
+                near = [h for h in (k - 1, k + 1) if h // levels == f]
+                beside = [g_ref[t, h * 8 : h * 8 + 8, :] for h in near]
+                out = own[len(near)] * q + mix * sum(beside[1:], beside[0])
+                out = out + ae * e - aw * w + an * nn - as_ * s
                 go_ref[t, k * 8 : k * 8 + 8, :] = out
         return carry
 
-    lax.fori_loop(0, tiles, fine, 0)
-
+    gn_in.wait()
+    lax.fori_loop(0, tiles, fine, 0, unroll=2)
+
+    ti_in.wait()
     for c in halo:
         c.wait_recv()
 
@@ -228,21 +249,22 @@
             count = count + jnp.where(rows == col_recv[d, c], 1.0, 0.0)
     keep = 1.0 - (time_step * coarse_penalty) * count
 
-    def glue(k, carry):
-        total = jnp.zeros((columns, LANES), jnp.float32)
+    def glue(f, carry):
+        total = [jnp.zeros((columns, LANES), jnp.float32)] * levels
         for d in range(ngx):
             for c in range(CAP):
-                row = tr_recv[d, c, pl.ds(k, 1), :]
-                total = total + jnp.where(
-                    rows == col_recv[d, c], jnp.broadcast_to(row, (columns, LANES)), 0.0
-                )
-        at = pl.multiple_of(k * columns, columns)
-        fo_ref[pl.ds(at, columns), :] = (
-            keep * f_ref[pl.ds(at, columns), :] + (time_step * coarse_penalty) * total
-        )
+                here = rows == col_recv[d, c]
+                for z in range(levels):
+                    row = tr_recv[d, c, pl.ds(f * levels + z, 1), :]
+                    total[z] = total[z] + jnp.where(here, jnp.broadcast_to(row, (columns, LANES)), 0.0)
+        for z in range(levels):
+            at = pl.multiple_of((f * levels + z) * columns, columns)
+            fo_ref[pl.ds(at, columns), :] = (
+                keep * f_ref[pl.ds(at, columns), :] + (time_step * coarse_penalty) * total[z]
+            )
         return carry
 
-    lax.fori_loop(0, nz, glue, 0)
+    lax.fori_loop(0, nfield, glue, 0)
 
     def around(q, k):
         e = jnp.where(rows == columns - 1, hx_recv[1, k : k + 1, :], pltpu.roll(q, columns - 1, 0))
@@ -291,7 +313,7 @@
             go_ref[t, k * 8 : k * 8 + 8, :] = go_ref[t, k * 8 : k * 8 + 8, :] + add
         return carry
 
-    lax.fori_loop(0, tiles, settle, 0)
+    lax.fori_loop(0, tiles, settle, 0, unroll=4)
 
     for c in col + halo + traces + answers:
         c.wait_send()
@@ -328,7 +350,6 @@
     g = halves_in(fine_fields).reshape(tiles, nz * 8, LANES)
     gn = halves_in(fine_viscosity).reshape(tiles, levels * 8, LANES)
     vmem = pl.BlockSpec(memory_space=pltpu.VMEM)
-    smem = pl.BlockSpec(memory_space=pltpu.SMEM)
     dma = pltpu.SemaphoreType.DMA
     trace = pltpu.VMEM((ngx, CAP, nz, LANES), f32)
     fo, go = pl.pallas_call(
@@ -337,9 +358,18 @@
             jax.ShapeDtypeStruct((nz * columns, span), f32),
             jax.ShapeDtypeStruct((tiles, nz * 8, LANES), f32),
         ),
-        in_specs=[vmem] * 6 + [smem] * 2,
+        in_specs=[pl.BlockSpec(memory_space=pltpu.HBM)] * 8,
         out_specs=(vmem, vmem),
         scratch_shapes=[
+            pltpu.VMEM((nz * columns, span), f32),
+            pltpu.VMEM((levels * columns, span), f32),
+            pltpu.VMEM(precursor.shape, f32),
+            pltpu.VMEM((1, tile_index.shape[0]), i32),
+            pltpu.VMEM(g.shape, f32),
+            pltpu.VMEM(gn.shape, f32),
+            pltpu.SMEM(partner_gx.shape, i32),
+            pltpu.SMEM(partner_col.shape, i32),
+            dma((8,)),
             pltpu.SMEM((ngx, CAP), i32),
             pltpu.SMEM((ngx, LANES), i32),
             pltpu.SMEM((ngx, LANES), i32),
@@ -356,13 +386,13 @@
         compiler_params=pltpu.CompilerParams(
             collective_id=0, has_side_effects=True, vmem_limit_bytes=40 * 2**20
         ),
-    )(
+    )(*(pltpu.with_memory_space_constraint(a, pltpu.HBM) for a in (
         fields.reshape(nz * columns, span),
         viscosity.reshape(levels * columns, span),
         precursor,
         tile_index.reshape(1, -1),
         g, gn, partner_gx, partner_col,
-    )
+    )))
     fine_out = halves_out(go.reshape(tiles, nfield, levels, 8, LANES))
     return fo.reshape(fields.shape), fine_out
 

time: 29.6 us -> 20 us (0.68)
  local copies, waits for them, and re-layouts: 8.52 us -> 1.78 us
  Pallas kernels: 20.1 us -> 17.5 us
    unnamed x18 -> x2, local copies, waits for them, and re-layouts: 8.52 us -> 1.78 us
    pallas_call x1, Pallas kernels: 20.1 us -> 17.5 us  [on_device(): pl.pallas_call(functools.partial(kernel, ngx, ngy, nfield, levels, column...]
where the time goes in v1:
time: 20 us; the launch traced here: 19.9 us
  Pallas kernels  17.5 us (88%)
  local copies, waits for them, and re-layouts  1.78 us (9%)
  between operations  0.64 us (3%)
    pallas_call x1, Pallas kernels, on_device(): pl.pallas_call(functools.partial(kernel, ngx, ngy, nfield, levels, column...  17.5 us
    unnamed x2, local copies, waits for them, and re-layouts  1.78 us

profile of v1, /device:TPU:0, one launch (start us, length us, event | category | flops | bytes accessed | tf_op | source)
XLA Modules:
  0.0 19.9 jit_solution(12489848584363525533)
XLA Ops:
  0.6 17.5 %shard_map.95 = (f32[640,128]{1,0:T(8,128)S(1)}, f32[16,160,128]{2,1,0:T(8,128)S(1)}) custom-call(f32[640,128]{1,0:T(8,128)} %bitcast.22, f32[128,128]{1,0:T(8,128)} %bitcast.24, f32[5,4,128]{2,1,0:T(4,128)} %p_hbm.1, s32[1,128]{1,0:T(1,128)} %bitcast.25, f32[16,160,128]{2,1,0:T(8,128)} %bitcast.21, f32[16,32,128]{2,1,0:T(8,128)} %bitcast.23, s32[16]{0:T(128)} %pgx_hbm.1, ...), custom_call_target="tpu_custom_call" | custom-call | tf_op jit(solution)/shard_map/pallas_call | solution.py:355
  18.1 0.7 %copy.15 = f32[5,4,32,128]{3,2,1,0:T(8,128)} copy(f32[5,4,32,128]{3,2,1,0:T(8,128)S(1)} %bitcast.20) | data formatting | bytes 655360
  18.8 1.1 %copy.16 = f32[16,5,4,4,256]{4,3,2,1,0:T(4,128)} copy(f32[16,5,4,4,256]{4,3,2,1,0:T(4,128)S(1)} %bitcast.19) | data formatting | bytes 2621440

commit v2 on v1

--- a/solution.py
+++ b/solution.py
@@ -23,7 +23,7 @@
 def kernel(
     ngx, ngy, nfield, levels, columns, tiles, width,
     f_hbm, n_hbm, p_hbm, ti_hbm, g_hbm, gn_hbm, pgx_hbm, pcol_hbm,
-    fo_ref, go_ref,
+    fo_ref, go_ref, at_ref,
     f_ref, n_ref, p_ref, ti_ref, g_ref, gn_ref, pgx_ref, pcol_ref, in_sems,
     tid, col_send, col_recv, ctr, tr_send, tr_recv, an_send, an_recv,
     hx_send, hx_recv, hy_send, hy_recv, pr,
@@ -158,12 +158,11 @@
             col[d - 1].wait_recv()
         for c in range(CAP):
             at = jnp.maximum(col_recv[d, c], 0)
-            for k in range(nz):
-                row = f_ref[pl.ds(k * columns + at, 1), :]
-                if d:
-                    an_send[d, c, k : k + 1, :] = row
-                else:
-                    an_recv[0, c, k : k + 1, :] = row
+            found = f_ref[pl.ds(at, nz, stride=columns), :]
+            if d:
+                an_send[d, c] = found
+            else:
+                an_recv[0, c] = found
         if d:
             answers[d - 1].start()
 
@@ -294,34 +293,47 @@
 
     for c in answers:
         c.wait_recv()
+    for t in range(tiles):
+        d = lax.rem(pgx_ref[t] - mx + ngx, ngx)
+        at_ref[t] = an_recv[d, jnp.where(tid[d, 0] == t, 0, 1)]
+
+    for c in col + halo + traces + answers:
+        c.wait_send()
+
+    @pl.when(mx == 0)
+    def _():
+        for c in plane:
+            c.wait_send()
+
+
+def settle_kernel(nz, chunk, fo_ref, go_ref, at_ref, fo_hbm, go_hbm, done, sems):
+    tiles = go_ref.shape[0]
+    outer = pltpu.make_async_copy(fo_ref, fo_hbm, sems.at[tiles // chunk])
+    outer.start()
+    lane_z = lax.broadcasted_iota(jnp.int32, (nz, LANES), 1)
+    row8 = lax.broadcasted_iota(jnp.int32, (8, LANES), 0)
+    is_glue, first_half = (row8 % 4) == 0, row8 < 4
     low = lane_z // 2
     low_up = low + lane_z % 2
     high = low + LANES // 2
     high_up = jnp.minimum(low_up + LANES // 2, LANES - 1)
-
-    def settle(t, carry):
-        goal = pgx_ref[t]
-        d = lax.rem(goal - mx + ngx, ngx)
-        c = jnp.where(tid[d, 0] == t, 0, 1)
-        a = (0.5 * time_step * fine_penalty) * an_recv[d, c]
-        r0 = lane_take(a, low) + lane_take(a, low_up)
-        r1 = lane_take(a, high) + lane_take(a, high_up)
-        for k in range(nz):
-            b0 = jnp.broadcast_to(r0[k : k + 1, :], (8, LANES))
-            b1 = jnp.broadcast_to(r1[k : k + 1, :], (8, LANES))
-            add = jnp.where(is_glue, jnp.where(row8 < 4, b0, b1), zero)
-            go_ref[t, k * 8 : k * 8 + 8, :] = go_ref[t, k * 8 : k * 8 + 8, :] + add
-        return carry
-
-    lax.fori_loop(0, tiles, settle, 0, unroll=4)
-
-    for c in col + halo + traces + answers:
-        c.wait_send()
-
-    @pl.when(mx == 0)
-    def _():
-        for c in plane:
-            c.wait_send()
+    copies = []
+    for j in range(tiles // chunk):
+        for t in range(j * chunk, (j + 1) * chunk):
+            a = (0.5 * time_step * fine_penalty) * at_ref[t]
+            r0 = lane_take(a, low) + lane_take(a, low_up)
+            r1 = lane_take(a, high) + lane_take(a, high_up)
+            for k in range(nz):
+                b0 = jnp.broadcast_to(r0[k : k + 1, :], (8, LANES))
+                b1 = jnp.broadcast_to(r1[k : k + 1, :], (8, LANES))
+                add = jnp.where(is_glue, jnp.where(first_half, b0, b1), 0.0)
+                done[t, k * 8 : k * 8 + 8, :] = go_ref[t, k * 8 : k * 8 + 8, :] + add
+        part = pl.ds(j * chunk, chunk)
+        copies.append(pltpu.make_async_copy(done.at[part], go_hbm.at[part], sems.at[j]))
+        copies[-1].start()
+    for c in copies:
+        c.wait()
+    outer.wait()
 
 
 def halves_in(a):
@@ -352,14 +364,15 @@
     vmem = pl.BlockSpec(memory_space=pltpu.VMEM)
     dma = pltpu.SemaphoreType.DMA
     trace = pltpu.VMEM((ngx, CAP, nz, LANES), f32)
-    fo, go = pl.pallas_call(
+    fo, go, answer = pl.pallas_call(
         functools.partial(kernel, ngx, ngy, nfield, levels, columns, tiles, width),
         out_shape=(
             jax.ShapeDtypeStruct((nz * columns, span), f32),
             jax.ShapeDtypeStruct((tiles, nz * 8, LANES), f32),
+            jax.ShapeDtypeStruct((tiles, nz, LANES), f32),
         ),
         in_specs=[pl.BlockSpec(memory_space=pltpu.HBM)] * 8,
-        out_specs=(vmem, vmem),
+        out_specs=(vmem, vmem, vmem),
         scratch_shapes=[
             pltpu.VMEM((nz * columns, span), f32),
             pltpu.VMEM((levels * columns, span), f32),
@@ -393,6 +406,16 @@
         tile_index.reshape(1, -1),
         g, gn, partner_gx, partner_col,
     )))
+    chunk = 4
+    hbm = pl.BlockSpec(memory_space=pltpu.HBM)
+    fo, go = pl.pallas_call(
+        functools.partial(settle_kernel, nz, chunk),
+        out_shape=(pltpu.HBM(fo.shape, f32), pltpu.HBM(go.shape, f32)),
+        in_specs=[vmem] * 3,
+        out_specs=(hbm, hbm),
+        scratch_shapes=[pltpu.VMEM(go.shape, f32), dma((tiles // chunk + 1,))],
+        compiler_params=pltpu.CompilerParams(vmem_limit_bytes=20 * 2**20),
+    )(fo, go, answer)
     fine_out = halves_out(go.reshape(tiles, nfield, levels, 8, LANES))
     return fo.reshape(fields.shape), fine_out
 

time: 20 us -> 18.9 us (0.945)
  local copies, waits for them, and re-layouts: 1.78 us -> 0 us
  Pallas kernels: 17.5 us -> 18.1 us
    unnamed x2 -> x0, local copies, waits for them, and re-layouts: 1.78 us -> none
    pallas_call x0 -> x1, Pallas kernels: none -> 1.31 us  [on_device(): pl.pallas_call(functools.partial(settle_kernel, nz, chunk), out_shape=(pl...]
    pallas_call x1, Pallas kernels: 17.5 us -> 16.8 us  [on_device(): pl.pallas_call(functools.partial(kernel, ngx, ngy, nfield, levels, column...]
where the time goes in v2:
time: 18.9 us; the launch traced here: 18.7 us
  Pallas kernels  18.1 us (96%)
  between operations  0.64 us (3%)
    pallas_call x1, Pallas kernels, on_device(): pl.pallas_call(functools.partial(kernel, ngx, ngy, nfield, levels, column...  16.8 us
    pallas_call x1, Pallas kernels, on_device(): pl.pallas_call(functools.partial(settle_kernel, nz, chunk), out_shape=(pl...  1.31 us

profile of v2, /device:TPU:0, one launch (start us, length us, event | category | flops | bytes accessed | tf_op | source)
XLA Modules:
  0.0 18.7 jit_solution(5303611748205838934)
XLA Ops:
  0.6 16.8 %shard_map.95 = (f32[640,128]{1,0:T(8,128)S(1)}, f32[16,160,128]{2,1,0:T(8,128)S(1)}, f32[16,20,128]{2,1,0:T(8,128)S(1)}) custom-call(f32[640,128]{1,0:T(8,128)} %bitcast.20, f32[128,128]{1,0:T(8,128)} %bitcast.22, f32[5,4,128]{2,1,0:T(4,128)} %p_hbm.1, s32[1,128]{1,0:T(1,128)} %bitcast.23, f32[16,160,128]{2,1,0:T(8,128)} %bitcast.19, ...), custom_call_target="tpu_custom_call" | custom-call | tf_op jit(solution)/shard_map/pallas_call | solution.py:367
  17.4 1.3 %shard_map.96 = (f32[640,128]{1,0:T(8,128)}, f32[16,160,128]{2,1,0:T(8,128)}) custom-call(f32[640,128]{1,0:T(8,128)S(1)} %get-tuple-element.7.fo_ref, f32[16,160,128]{2,1,0:T(8,128)S(1)} %get-tuple-element.8.go_ref, f32[16,20,128]{2,1,0:T(8,128)S(1)} %get-tuple-element.9.at_ref), custom_call_target="tpu_custom_call" | custom-call | tf_op jit(solution)/shard_map/pallas_call | solution.py:411
